TPU v7x, 32 devices: a whole 2x2x4 slice. The times are simulated.
32 devices in a mesh: kpair: 4 (over x, core), band: 2 (over y), pencil: 4 (over z).
Axes of the slice: x: 2, y: 2, z: 4, core: 2. Of those that a mesh axis runs over, the one named last changes fastest.
Arguments:
- orbitals: float32 [2, 4, 2, 96, 9216], P(None, 'kpair', 'band', 'pencil'), may hold values from -6 to 6
- kcoords: int32 [4, 3], replicated, may hold values from 0 to 3, as said below
Outputs:
- exchange_vectors: float32 [2, 4, 2, 96, 9216], P(None, 'kpair', 'band', 'pencil')
Inputs may be any that keep to these rules, and one draw needn't show every extreme that they name: `kcoords`: each row is a point of a 4 x 4 x 4 k-point grid given by three integer coordinates; the rows are distinct.
All inputs are finite; a program needn't handle non-finite values.
Results may differ from a plain program's by a relative error of at most 0.0001.
Values sent between devices are 32-bit elements; how exact they have to be, the bound alone decides.
A program may use at most 128 MiB of HBM per device.

v0:
```python
import math

import jax
import jax.numpy as jnp
from jax import lax
from jax.sharding import PartitionSpec as P

GRID = 96
NB = 2


screening = 0.5


def frequencies():
    positions = jnp.arange(GRID)
    return jnp.where(positions < GRID // 2, positions, positions - GRID).astype(jnp.float32)


def coulomb_grid(shift_vector, along_x, along_y, along_z):
    squared = (along_x[:, None, None] + shift_vector[0]) ** 2
    squared = squared + (along_y[None, :, None] + shift_vector[1]) ** 2
    squared = squared + (along_z[None, None, :] + shift_vector[2]) ** 2
    radius = GRID // 2 - 1
    factor = (2.0 * math.pi / GRID) ** 2
    return jnp.where(
        squared <= radius * radius, 4.0 * math.pi / (factor * squared + screening), 0.0
    )


def tables():
    positions = jnp.arange(GRID, dtype=jnp.int32)
    product = positions[:, None] * positions[None, :] % GRID
    angle = product.astype(jnp.float32) * (2.0 * math.pi / GRID)
    return (jnp.cos(angle), jnp.sin(angle))


def transform(fields, pattern, cosine_table, sine_table, inverse):
    with_cos = jnp.einsum(pattern, fields, cosine_table, precision=lax.Precision.HIGHEST)
    with_sin = jnp.einsum(pattern, fields, sine_table, precision=lax.Precision.HIGHEST)
    if inverse:
        real_part = with_cos[0] - with_sin[1]
        imag_part = with_cos[1] + with_sin[0]
    else:
        real_part = with_cos[0] + with_sin[1]
        imag_part = with_cos[1] - with_sin[0]
    return jnp.stack([real_part, imag_part])


def apply_pairs(own_orbitals, far_orbitals, shift_vector, with_reverse, weight):
    band_local = own_orbitals.shape[1]
    far_bands = far_orbitals.shape[1]
    slab_rows = own_orbitals.shape[2]
    cosine_table, sine_table = tables()
    frequency = frequencies()
    slab_cols = GRID // lax.axis_size("pencil")
    pencil_index = lax.axis_index("pencil")
    local_y = lax.dynamic_slice_in_dim(frequency, pencil_index * slab_cols, slab_cols)
    coulomb = coulomb_grid(shift_vector, frequency, local_y, frequency) * (1.0 / GRID**3)
    own_real = own_orbitals[0][:, None]
    own_imag = own_orbitals[1][:, None]
    far_real = far_orbitals[0][None]
    far_imag = far_orbitals[1][None]
    density_real = far_real * own_real + far_imag * own_imag
    density_imag = far_real * own_imag - far_imag * own_real
    density = jnp.stack([density_real, density_imag]).reshape(
        2, band_local * far_bands, slab_rows, GRID, GRID
    )
    density = transform(density, "cbxyn,nm->cbxym", cosine_table, sine_table, False)
    density = transform(density, "cbxnz,nm->cbxmz", cosine_table, sine_table, False)
    spectrum = transform(
        lax.all_to_all(density, "pencil", split_axis=3, concat_axis=2, tiled=True),
        "cbnyz,nm->cbmyz",
        cosine_table,
        sine_table,
        False,
    )
    spectrum = spectrum * coulomb
    filtered = transform(spectrum, "cbnyz,nm->cbmyz", cosine_table, sine_table, True)
    potential = lax.all_to_all(filtered, "pencil", split_axis=2, concat_axis=3, tiled=True)
    potential = transform(potential, "cbxnz,nm->cbxmz", cosine_table, sine_table, True)
    potential = transform(potential, "cbxyn,nm->cbxym", cosine_table, sine_table, True)
    potential = potential.reshape(2, band_local, far_bands, slab_rows, GRID * GRID)
    pot_real = potential[0]
    pot_imag = potential[1]
    direct = weight * jnp.stack(
        [
            jnp.sum(far_real * pot_real - far_imag * pot_imag, axis=1),
            jnp.sum(far_real * pot_imag + far_imag * pot_real, axis=1),
        ]
    )
    if not with_reverse:
        return (direct, None)
    reverse = weight * jnp.stack(
        [
            jnp.sum(own_real * pot_real + own_imag * pot_imag, axis=0),
            jnp.sum(own_imag * pot_real - own_real * pot_imag, axis=0),
        ]
    )
    return (direct, reverse)


def body(orbitals, kcoords):
    kpts = kcoords.shape[0]
    band_local = orbitals.shape[2]
    slab_rows = orbitals.shape[3]
    plane = orbitals.shape[4]
    weight = -1.0 / (kpts * NB)
    coords = kcoords.astype(jnp.float32) * 0.25
    kpoint_index = lax.axis_index("kpair")
    band_index = lax.axis_index("band")
    own_orbitals = orbitals[:, 0]
    own_coords = coords[kpoint_index]
    empty = jnp.zeros((2, band_local, slab_rows, plane), jnp.float32)
    everyone = lax.all_gather(own_orbitals, ("kpair", "band"), axis=1, tiled=True)
    partial_value = jnp.zeros((2, kpts * NB, slab_rows, plane), jnp.float32)
    own_sum = empty
    for offset in range(kpts):
        if 2 * offset <= kpts:
            target = (kpoint_index + offset) % kpts
            far_orbitals = lax.dynamic_slice_in_dim(everyone, target * NB, NB, 1)
            direct, reverse = apply_pairs(
                own_orbitals,
                far_orbitals,
                own_coords - coords[target],
                0 < 2 * offset < kpts,
                weight,
            )
            own_sum = own_sum + direct
            if reverse is not None:
                current = lax.dynamic_slice_in_dim(partial_value, target * NB, NB, 1)
                partial_value = lax.dynamic_update_slice_in_dim(
                    partial_value, reverse, target * NB, 1
                )
    own_start = kpoint_index * NB + band_index * band_local
    current = lax.dynamic_slice_in_dim(partial_value, own_start, band_local, 1)
    partial_value = lax.dynamic_update_slice_in_dim(partial_value, current + own_sum, own_start, 1)
    result = lax.psum_scatter(partial_value, ("kpair", "band"), scatter_dimension=1, tiled=True)
    return result.reshape(2, 1, band_local, slab_rows, plane)


def solution(mesh):
    in_specs = (P(None, "kpair", "band", "pencil", None), P())
    out_specs = P(None, "kpair", "band", "pencil", None)
    return jax.shard_map(body, mesh=mesh, in_specs=in_specs, out_specs=out_specs, check_vma=False)
```

profile of v0, /device:TPU:0, one launch (start us, length us, event | category | flops | bytes accessed | tf_op | source)
XLA Modules:
  0.0 960.1 jit_solution(9675833647412973116)
XLA Ops:
  8.1 82.6 %all-gather.3.cloned.1.call-done = f32[2,8,1,24,9216]{4,3,1,2,0:T(8,128)} async-done(((f32[2,1,1,24,9216]{4,3,1,2,0:T(8,128)}), f32[2,8,1,24,9216]{4,3,1,2,0:T(8,128)}) %all-gather.3.cloned.1.call-update) | async-done | bytes 14155792 | tf_op jit(solution)/shard_map/all_gather | solution.py:115
  90.8 6.4 fusion.42
  99.4 3.8 stack.68
  105.2 4.2 fusion.86
  109.4 4.2 fusion.103
  114.6 5.0 fusion.26
  119.7 4.8 fusion.25
  126.0 4.9 copy.59
  130.9 5.3 all-to-all-start
  141.7 99.3 %all-to-all-done = f32[2,2,24,96,96]{4,2,1,0,3:T(8,128)} async-done(((f32[2,2,24,96,96]{4,2,1,0,3:T(8,128)}), f32[2,2,24,96,96]{4,2,1,0,3:T(8,128)}, u32[]{:S(2)}, u32[]{:S(2)}) %all-to-all-start) | async-done | bytes 3538976 | tf_op jit(solution)/shard_map/all_to_all | solution.py:72
  244.0 4.7 convolution_bitcast_fusion.10
  248.7 4.7 convolution_bitcast_fusion.11
  254.5 5.1 fusion.32
  259.6 4.6 fusion.31
  265.6 5.0 copy.65
  270.7 5.0 all-to-all-start.1
  283.2 4.2 fusion.83
  287.5 4.2 fusion.100
  292.7 5.3 fusion.28
  297.9 4.8 fusion.27
  304.2 4.9 copy.81
  309.1 70.9 %all-to-all-done.1 = f32[2,2,96,24,96]{4,3,1,0,2:T(8,128)} async-done(((f32[2,2,96,24,96]{4,3,1,0,2:T(8,128)}), f32[2,2,96,24,96]{4,3,1,0,2:T(8,128)}, u32[]{:S(2)}, u32[]{:S(2)}) %all-to-all-start.1) | async-done | bytes 3538976 | tf_op jit(solution)/shard_map/all_to_all | solution.py:80
  380.0 5.1 all-to-all-start.2
  388.0 4.7 convolution_bitcast_fusion.8
  392.8 4.7 convolution_bitcast_fusion.9
  398.5 4.7 fusion.8
  403.2 4.3 fusion.9
  416.1 5.2 multiply_subtract_fusion
  430.7 4.2 fusion.80
  434.9 4.2 fusion.97
  440.1 5.1 fusion.30
  445.2 4.8 fusion.29
  451.5 4.8 copy.93
  456.3 32.6 %all-to-all-done.2 = f32[2,2,24,96,96]{4,2,1,0,3:T(8,128)} async-done(((f32[2,2,24,96,96]{4,2,1,0,3:T(8,128)}), f32[2,2,24,96,96]{4,2,1,0,3:T(8,128)}, u32[]{:S(2)}, u32[]{:S(2)}) %all-to-all-start.2) | async-done | bytes 3538976 | tf_op jit(solution)/shard_map/all_to_all | solution.py:72
  488.8 5.4 all-to-all-start.4
  498.8 4.7 convolution_bitcast_fusion.6
  503.6 4.7 convolution_bitcast_fusion.7
  509.3 4.7 fusion.34
  514.0 4.6 fusion.33
  520.1 5.3 copy.87
  525.4 72.4 %all-to-all-done.4 = f32[2,2,24,96,96]{4,2,1,0,3:T(8,128)} async-done(((f32[2,2,24,96,96]{4,2,1,0,3:T(8,128)}), f32[2,2,24,96,96]{4,2,1,0,3:T(8,128)}, u32[]{:S(2)}, u32[]{:S(2)}) %all-to-all-start.4) | async-done | bytes 3538976 | tf_op jit(solution)/shard_map/all_to_all | solution.py:72
  597.8 4.9 all-to-all-start.3
  607.3 4.7 convolution_bitcast_fusion.2
  612.1 4.7 convolution_bitcast_fusion.3
  617.8 4.7 fusion.36
  622.5 4.6 fusion.35
  628.6 5.0 copy.99
  633.6 73.0 %all-to-all-done.3 = f32[2,2,96,24,96]{4,3,1,0,2:T(8,128)} async-done(((f32[2,2,96,24,96]{4,3,1,0,2:T(8,128)}), f32[2,2,96,24,96]{4,3,1,0,2:T(8,128)}, u32[]{:S(2)}, u32[]{:S(2)}) %all-to-all-start.3) | async-done | bytes 3538976 | tf_op jit(solution)/shard_map/all_to_all | solution.py:80
  706.6 5.0 all-to-all-start.5
  714.6 4.7 convolution_bitcast_fusion.4
  719.3 4.7 convolution_bitcast_fusion.5
  725.1 4.7 fusion.4
  729.8 4.3 fusion.5
  740.7 3.7 sub.189
  744.4 8.6 subtract_reduce_fusion
  753.1 6.8 broadcast_in_dim.8
  761.9 53.6 %all-to-all-done.5 = f32[2,2,96,24,96]{4,3,1,0,2:T(8,128)} async-done(((f32[2,2,96,24,96]{4,3,1,0,2:T(8,128)}), f32[2,2,96,24,96]{4,3,1,0,2:T(8,128)}, u32[]{:S(2)}, u32[]{:S(2)}) %all-to-all-start.5) | async-done | bytes 3538976 | tf_op jit(solution)/shard_map/all_to_all | solution.py:80
  818.4 4.7 convolution_bitcast_fusion
  823.2 5.0 convolution_bitcast_fusion.1
  829.1 4.3 fusion
  833.4 4.3 fusion.1
  840.2 3.8 sub.200
  846.5 4.1 fusion.50
  853.9 99.1 %reduce-scatter.2.cloned.1.call-done = f32[2,1,24,9216]{3,2,0,1:T(8,128)} async-done(((f32[2,8,24,9216]{3,2,0,1:T(8,128)}), f32[2,1,24,9216]{3,2,0,1:T(8,128)}) %reduce-scatter.2.cloned.1.call-update) | async-done | bytes 1769488 | tf_op jit(solution)/shard_map/reduce_scatter | solution.py:138
  (92 shorter events, 92.1 us)
Async XLA Ops:
  6.5 1.5 copy-start.4
  6.5 84.2 %all-gather.3.cloned.1.call-start = ((), (), s32[]{:S(2)}) async-start(), calls=%async_computation.8 | async-start | bytes 15925248 | tf_op jit(solution)/shard_map/all_gather | solution.py:115
  8.1 89.1 %copy-start = (f32[24,9216]{1,0:T(8,128)}, f32[24,9216]{1,0:T(8,128)S(1)}, u32[]{:S(2)}) copy-start(f32[24,9216]{1,0:T(8,128)S(1)} %get-tuple-element.57) | copy-start | bytes 2654212
  8.1 89.0 %copy-start.1 = (f32[24,9216]{1,0:T(8,128)}, f32[24,9216]{1,0:T(8,128)S(1)}, u32[]{:S(2)}) copy-start(f32[24,9216]{1,0:T(8,128)S(1)} %get-tuple-element.58) | copy-start | bytes 2654212
  130.9 5.3 copy-start.9
  130.9 110.2 %all-to-all-start = ((f32[2,2,24,96,96]{4,2,1,0,3:T(8,128)}), f32[2,2,24,96,96]{4,2,1,0,3:T(8,128)}, u32[]{:S(2)}, u32[]{:S(2)}) async-start(f32[2,2,24,96,96]{4,2,1,0,3:T(8,128)} %copy.59), calls=%async_computation | async-start | bytes 9437184 | tf_op jit(solution)/shard_map/all_to_all | solution.py:72
  270.7 109.3 %all-to-all-start.1 = ((f32[2,2,96,24,96]{4,3,1,0,2:T(8,128)}), f32[2,2,96,24,96]{4,3,1,0,2:T(8,128)}, u32[]{:S(2)}, u32[]{:S(2)}) async-start(f32[2,2,96,24,96]{4,3,1,0,2:T(8,128)} %copy.65), calls=%async_computation.1 | async-start | bytes 9437184 | tf_op jit(solution)/shard_map/all_to_all | solution.py:80
  380.0 108.9 %all-to-all-start.2 = ((f32[2,2,24,96,96]{4,2,1,0,3:T(8,128)}), f32[2,2,24,96,96]{4,2,1,0,3:T(8,128)}, u32[]{:S(2)}, u32[]{:S(2)}) async-start(f32[2,2,24,96,96]{4,2,1,0,3:T(8,128)} %copy.81), calls=%async_computation.2 | async-start | bytes 9437184 | tf_op jit(solution)/shard_map/all_to_all | solution.py:72
  428.1 2.4 copy-start.2
  488.8 108.9 %all-to-all-start.4 = ((f32[2,2,24,96,96]{4,2,1,0,3:T(8,128)}), f32[2,2,24,96,96]{4,2,1,0,3:T(8,128)}, u32[]{:S(2)}, u32[]{:S(2)}) async-start(f32[2,2,24,96,96]{4,2,1,0,3:T(8,128)} %copy.93), calls=%async_computation.4 | async-start | bytes 9437184 | tf_op jit(solution)/shard_map/all_to_all | solution.py:72
  525.4 78.5 %copy-start.10 = (f32[24]{0:T(128)S(1)}, f32[24]{0:T(128)}, u32[]{:S(2)}) copy-start(f32[24]{0:T(128)} %get-tuple-element.65) | copy-start | bytes 292
  597.8 108.9 %all-to-all-start.3 = ((f32[2,2,96,24,96]{4,3,1,0,2:T(8,128)}), f32[2,2,96,24,96]{4,3,1,0,2:T(8,128)}, u32[]{:S(2)}, u32[]{:S(2)}) async-start(f32[2,2,96,24,96]{4,3,1,0,2:T(8,128)} %copy.87), calls=%async_computation.3 | async-start | bytes 9437184 | tf_op jit(solution)/shard_map/all_to_all | solution.py:80
  706.6 108.9 %all-to-all-start.5 = ((f32[2,2,96,24,96]{4,3,1,0,2:T(8,128)}), f32[2,2,96,24,96]{4,3,1,0,2:T(8,128)}, u32[]{:S(2)}, u32[]{:S(2)}) async-start(f32[2,2,96,24,96]{4,3,1,0,2:T(8,128)} %copy.99), calls=%async_computation.5 | async-start | bytes 9437184 | tf_op jit(solution)/shard_map/all_to_all | solution.py:80
  711.6 241.4 %reduce-scatter.2.cloned.1.call-start = ((), (), s32[]{:S(2)}) async-start(), calls=%async_computation.7 | async-start | bytes 15925248 | tf_op jit(solution)/shard_map/reduce_scatter | solution.py:138
  753.1 6.8 copy-start.3
  846.5 4.2 copy-start.5
  846.5 4.2 copy-start.6
  846.5 4.2 copy-start.7
  846.5 4.2 copy-start.8
Sparse Core Ops, SparseCore 0:
  9.3 81.4 all-gather.2
  854.0 98.9 reduce-scatter.1
where the time goes:
time: 964 us; the launch traced here: 960 us
  waiting for transfers between devices  584 us (61%)
  matrix products  167 us (17%)
  local copies, waits for them, and re-layouts  100 us (10%)
  other arithmetic  63.4 us (7%)
  starting transfers between devices  30.7 us (3%)
  between operations  14.6 us (2%)
    all_to_all x3, waiting for transfers between devices, apply_pairs(): lax.all_to_all(density, 'pencil', split_axis=3, concat_axis=2, tiled=True)  204 us
    all_to_all x3, waiting for transfers between devices, apply_pairs(): lax.all_to_all(filtered, 'pencil', split_axis=2, concat_axis=3, tiled=True)  198 us
    reduce_scatter x1, waiting for transfers between devices, body(): lax.psum_scatter(partial_value, ('kpair', 'band'), scatter_dimension=1, t...  99.1 us
    dot_general x18, matrix products, transform(): jnp.einsum(pattern, fields, sine_table, precision=lax.Precision.HIGHEST)  84.6 us
    all_gather x1, waiting for transfers between devices, body(): lax.all_gather(own_orbitals, ('kpair', 'band'), axis=1, tiled=True)  82.6 us
    dot_general x18, matrix products, transform(): jnp.einsum(pattern, fields, cosine_table, precision=lax.Precision.HIGHEST)  82.2 us
    another operation x6, local copies, waits for them, and re-layouts, transform(): return jnp.stack([real_part, imag_part])  30 us
  transfers between devices with their start and end apart: 8, of which 8 were waited for; matrix products, arithmetic and copies ran while one was open for 23% of the time, Pallas kernels for 0%

commit v1 on v0

v1 whole, which is shorter than its diff:
```python
import functools
import math

import jax
import jax.numpy as jnp
import ml_dtypes
import numpy as np
from jax import lax
from jax.experimental import pallas as pl
from jax.experimental.pallas import tpu as pltpu
from jax.sharding import PartitionSpec as P

SCREENING = 0.5
CHUNKS = 4
LANES = 128
VMEM = 48 * 1024 * 1024


def splits(table):
    high = table.astype(np.float32).astype(ml_dtypes.bfloat16)
    low = (table - high.astype(np.float64)).astype(np.float32).astype(ml_dtypes.bfloat16)
    return jnp.asarray(high), jnp.asarray(low)


def tables(grid):
    n = np.arange(grid)
    angle = (n[:, None] * n[None, :] % grid) * (2.0 * math.pi / grid)
    c, s = np.cos(angle), np.sin(angle)
    left = np.block([[c, s], [-s, c]])
    left_inverse = np.block([[c, -s], [s, c]])
    padded = -(-grid // LANES) * LANES

    def right(sine):
        table = np.zeros((2 * padded, 2 * padded))
        table[:grid, :grid] = c
        table[:grid, padded : padded + grid] = -sine
        table[padded : padded + grid, :grid] = sine
        table[padded : padded + grid, padded : padded + grid] = c
        return table

    return [splits(t) for t in (left, left_inverse, right(s), right(-s))]


def halves(x):
    high = x.astype(jnp.bfloat16)
    return high, (x - high.astype(jnp.float32)).astype(jnp.bfloat16)


def dot(a, b):
    return jnp.dot(a, b, preferred_element_type=jnp.float32)


def product(a, b):
    return dot(a[0], b[0]) + (dot(a[0], b[1]) + dot(a[1], b[0]))


def density_kernel(flag_ref, high_ref, low_ref, own_ref, far_ref, out_ref):
    rows = own_ref.shape[1]
    gr, gi = own_ref[0], own_ref[1]
    hr, hi = far_ref[0], far_ref[1]
    packed = flag_ref[0] > 0
    real = jnp.where(packed, gr * gr + gi * gi, hr * gr + hi * gi)
    imag = jnp.where(packed, hr * hr + hi * hi, hr * gi - hi * gr)
    result = product(
        (high_ref[...], low_ref[...]), halves(jnp.concatenate([real, imag], axis=0))
    )
    out_ref[0] = result[:rows]
    out_ref[1] = result[rows:]


def apply_kernel(flag_ref, high_ref, low_ref, pot_ref, own_ref, far_ref, direct_ref, reverse_ref):
    rows = own_ref.shape[1]
    pot = product(
        (high_ref[...], low_ref[...]),
        halves(jnp.concatenate([pot_ref[0], pot_ref[1]], axis=0)),
    )
    vr, vi = pot[:rows], pot[rows:]
    gr, gi = own_ref[0], own_ref[1]
    hr, hi = far_ref[0], far_ref[1]
    packed = flag_ref[0] > 0
    direct_ref[0] = jnp.where(packed, gr * vr, hr * vr - hi * vi)
    direct_ref[1] = jnp.where(packed, gi * vr, hr * vi + hi * vr)
    reverse_ref[0] = jnp.where(packed, hr * vi, gr * vr + gi * vi)
    reverse_ref[1] = jnp.where(packed, hi * vi, gi * vr - gr * vi)


def filter_kernel(grid, scale, shift_ref, *refs):
    tables_refs, refs = refs[:8], refs[8:]
    left, left_inverse, right, right_inverse = [
        (tables_refs[2 * i][...], tables_refs[2 * i + 1][...]) for i in range(4)
    ]
    count = len(refs) // 2
    ins, outs = refs[:count], refs[count:]
    planes, part, padded = ins[0].shape[1:]
    columns = [
        jnp.concatenate([r[c, i] for c in range(2) for r in ins], axis=0) for i in range(planes)
    ]
    field = product(left, halves(jnp.concatenate(columns, axis=1)))

    def to_rows(f):
        return jnp.concatenate(
            [
                jnp.concatenate(
                    [
                        f[c * grid : (c + 1) * grid, i * padded : (i + 1) * padded]
                        for c in range(2)
                    ],
                    axis=1,
                )
                for i in range(planes)
            ],
            axis=0,
        )

    field = product(halves(to_rows(field)), right)

    def frequency(index):
        return jnp.where(index < grid // 2, index, index - grid).astype(jnp.float32)

    first = pl.program_id(0) * planes
    ky = frequency(lax.broadcasted_iota(jnp.int32, (grid, padded), 0)) + shift_ref[1]
    kz = frequency(lax.broadcasted_iota(jnp.int32, (grid, padded), 1)) + shift_ref[2]
    radius = grid // 2 - 1
    factor = (2.0 * math.pi / grid) ** 2
    filters = []
    for i in range(planes):
        kx = frequency(jnp.full((grid, padded), first + i, jnp.int32)) + shift_ref[0]
        squared = kx * kx + ky * ky + kz * kz
        filters.append(
            jnp.where(
                squared <= radius * radius,
                (4.0 * math.pi * scale) / (factor * squared + SCREENING),
                0.0,
            )
        )
    coulomb = jnp.concatenate(filters, axis=0)
    field = field * jnp.concatenate([coulomb, coulomb], axis=1)
    field = product(halves(field), right_inverse)
    columns = [
        jnp.concatenate(
            [
                field[i * grid : (i + 1) * grid, c * padded : (c + 1) * padded]
                for c in range(2)
            ],
            axis=0,
        )
        for i in range(planes)
    ]
    field = product(left_inverse, halves(jnp.concatenate(columns, axis=1)))
    for c in range(2):
        for i in range(planes):
            for j, out in enumerate(outs):
                start = c * grid + j * part
                out[c, i] = field[start : start + part, i * padded : (i + 1) * padded]


def whole(array):
    return pl.BlockSpec(array.shape, lambda i: (0,) * array.ndim)


SCALARS = pl.BlockSpec(memory_space=pltpu.SMEM)


def lane_block(lanes):
    for parts in range(1, lanes + 1):
        if lanes % parts == 0 and lanes // parts % LANES == 0 and lanes // parts <= 1280:
            return lanes // parts
    return lanes


def along_x(kernel, results, flag, table, *fields):
    components, rows, lanes = fields[0].shape
    block = lane_block(lanes)
    spec = pl.BlockSpec((components, rows, block), lambda i: (0, 0, i))
    shape = jax.ShapeDtypeStruct((components, rows, lanes), jnp.float32)
    return pl.pallas_call(
        kernel,
        grid=(lanes // block,),
        in_specs=[SCALARS, whole(table[0]), whole(table[1])] + [spec] * len(fields),
        out_specs=[spec] * results,
        out_shape=[shape] * results,
        compiler_params=pltpu.CompilerParams(vmem_limit_bytes=VMEM),
        cost_estimate=pl.CostEstimate(
            flops=24 * rows * rows * lanes,
            bytes_accessed=8 * rows * lanes * (len(fields) + results),
            transcendentals=0,
        ),
    )(flag, *table, *fields)


def filtered(parts, shift, all_tables, grid, scale):
    planes = next(p for p in (8, 6, 4, 3, 2, 1) if grid % p == 0)
    flat = [t for pair in all_tables for t in pair]
    block = (2, planes) + parts[0].shape[2:]
    spec = pl.BlockSpec(block, lambda i: (0, i, 0, 0))
    return pl.pallas_call(
        functools.partial(filter_kernel, grid, scale),
        grid=(grid // planes,),
        in_specs=[SCALARS] + [whole(t) for t in flat] + [spec] * len(parts),
        out_specs=[spec] * len(parts),
        out_shape=[jax.ShapeDtypeStruct(p.shape, jnp.float32) for p in parts],
        compiler_params=pltpu.CompilerParams(vmem_limit_bytes=VMEM),
    )(shift, *flat, *parts)


def schedule(kpts, bands, sets):
    count = kpts * bands
    if count != 8 or bands != 2 or sets < 4:
        raise NotImplementedError
    x, core, y = 4, 2, 1
    rows = [
        (x, y | core, x | core, False),
        (x | core, y, core | y, False),
        (x | y, core, core | x, False),
        (x | y | core, core, core, True),
    ]
    partner = np.zeros((4, count), np.int32)
    packed = np.zeros((4, count), np.int32)
    for p, (even, odd, mask, diagonal) in enumerate(rows):
        for g in range(count):
            side = bin(g & mask).count("1") % 2
            partner[p, g] = g ^ (odd if side else even)
            packed[p, g] = int(diagonal and side == 1)
    return partner, packed


def body(orbitals, kcoords):
    kpts = kcoords.shape[0]
    bands = lax.axis_size("band") * orbitals.shape[2]
    pencils = lax.axis_size("pencil")
    slab, plane = orbitals.shape[3:]
    grid = slab * pencils
    count = kpts * bands
    partner, packed = schedule(kpts, bands, pencils)
    axes = ("kpair", "band", "pencil")
    pencil = lax.axis_index("pencil")
    orbital = lax.axis_index("kpair") * bands + lax.axis_index("band")
    row = pencil % 4
    far = jnp.asarray(partner)[row, orbital]
    flag = jnp.where(pencil < 4, jnp.asarray(packed)[row, orbital], 0).reshape(1)
    active = (pencil < 4).astype(jnp.float32)
    coords = kcoords.astype(jnp.float32) * 0.25
    shift = coords[orbital // bands] - coords[far // bands]
    shift = jnp.where(flag[0] > 0, 0.0, shift)
    fetch = [
        (int(partner[p % 4, g]) * pencils + p, g * pencils + p)
        for p in range(pencils)
        for g in range(count)
    ]
    give = [(b, a) for a, b in fetch]
    all_tables = tables(grid)
    padded = -(-grid // LANES) * LANES
    lanes = plane // CHUNKS
    part = lanes // grid

    own_chunks, far_chunks, spectra = [], [], []
    for j in range(CHUNKS):
        piece = orbitals[:, 0, 0, :, j * lanes : (j + 1) * lanes]
        own = lax.all_gather(piece, "pencil", axis=1, tiled=True)
        other = lax.ppermute(own, axes, fetch)
        own_chunks.append(own)
        far_chunks.append(other)
        (spectrum,) = along_x(density_kernel, 1, flag, all_tables[0], own, other)
        spectrum = spectrum.reshape(2, grid, part, grid)
        spectra.append(jnp.pad(spectrum, ((0, 0), (0, 0), (0, 0), (0, padded - grid))))

    scale = -1.0 / (count * grid**3)
    potentials = filtered(spectra, shift, all_tables, grid, scale)
    results = []
    for j in range(CHUNKS):
        potential = potentials[j][..., :grid].reshape(2, grid, lanes)
        direct, reverse = along_x(
            apply_kernel, 2, flag, all_tables[1], potential, own_chunks[j], far_chunks[j]
        )
        total = direct + lax.ppermute(reverse, axes, give)
        if pencils > 4:
            total = total * active
        results.append(lax.psum_scatter(total, "pencil", scatter_dimension=1, tiled=True))
    return jnp.concatenate(results, axis=2)[:, None, None]


def solution(mesh):
    in_specs = (P(None, "kpair", "band", "pencil", None), P())
    out_specs = P(None, "kpair", "band", "pencil", None)
    return jax.shard_map(body, mesh=mesh, in_specs=in_specs, out_specs=out_specs, check_vma=False)
```

time: 964 us -> 449 us (0.47)
  waiting for transfers between devices: 584 us -> 314 us
  matrix products: 167 us -> 0 us
  other arithmetic: 63.4 us -> 8.45 us
  local copies, waits for them, and re-layouts: 100 us -> 46.3 us
  Pallas kernels: 0 us -> 50.8 us
  starting transfers between devices: 30.7 us -> 11.7 us
    all_to_all x6 -> x0, waiting for transfers between devices: 402 us -> none  [the longest x3 204 us: apply_pairs(): lax.all_to_all(density, 'pencil', split_axis=3, concat_axis=2, tiled=True)]
    dot_general x36 -> x0, matrix products: 167 us -> none  [the longest x18 84.6 us: transform(): jnp.einsum(pattern, fields, sine_table, precision=lax.Precision.HIGHEST)]
    ppermute x0 -> x8, waiting for transfers between devices: none -> 81.1 us  [the longest x4 81.1 us: body(): total = direct + lax.ppermute(reverse, axes, give)]
    all_gather x1 -> x4, waiting for transfers between devices: 82.6 us -> 161 us  [body(): own = lax.all_gather(piece, 'pencil', axis=1, tiled=True)]
    pallas_call x0 -> x9, Pallas kernels: none -> 50.8 us  [the longest x1 27.7 us: filtered(): pl.pallas_call(functools.partial(filter_kernel, grid, scale), grid=(grid...]
    another operation x15 -> x0, local copies, waits for them, and re-layouts: 48.9 us -> none  [the longest x6 30 us: transform(): return jnp.stack([real_part, imag_part])]
    all_to_all x6 -> x0, starting transfers between devices: 30.6 us -> none  [the longest x3 15.8 us: apply_pairs(): lax.all_to_all(density, 'pencil', split_axis=3, concat_axis=2, tiled=True)]
    reduce_scatter x1 -> x4, waiting for transfers between devices: 99.1 us -> 70.3 us  [body(): lax.psum_scatter(total, 'pencil', scatter_dimension=1, tiled=True)]
  transfers between devices with their start and end apart: 8 -> 16, of which waited for: 8 -> 10; matrix products, arithmetic and copies ran while one was open for 23% -> 7% of each run, Pallas kernels for 0% -> 4%
where the time goes in v1:
time: 449 us; the launch traced here: 448 us
  waiting for transfers between devices  314 us (70%)
  Pallas kernels  50.8 us (11%)
  local copies, waits for them, and re-layouts  46.3 us (10%)
  between operations  17.1 us (4%)
  starting transfers between devices  11.7 us (3%)
  other arithmetic  8.45 us (2%)
    all_gather x4, waiting for transfers between devices, body(): own = lax.all_gather(piece, 'pencil', axis=1, tiled=True)  161 us
    ppermute x4, waiting for transfers between devices, body(): total = direct + lax.ppermute(reverse, axes, give)  81.1 us
    reduce_scatter x4, waiting for transfers between devices, body(): lax.psum_scatter(total, 'pencil', scatter_dimension=1, tiled=True)  70.3 us
    pallas_call x1, Pallas kernels, filtered(): pl.pallas_call(functools.partial(filter_kernel, grid, scale), grid=(grid...  27.7 us
    pallas_call x8, Pallas kernels, along_x(): pl.pallas_call(kernel, grid=(lanes // block,), in_specs=[SCALARS, whole(t...  23.1 us
    reshape x4, local copies, waits for them, and re-layouts, body(): spectrum = spectrum.reshape(2, grid, part, grid)  13.1 us
    pad x4, local copies, waits for them, and re-layouts, body(): jnp.pad(spectrum, ((0, 0), (0, 0), (0, 0), (0, padded - grid)))  11.7 us
  transfers between devices with their start and end apart: 16, of which 10 were waited for; matrix products, arithmetic and copies ran while one was open for 7% of the time, Pallas kernels for 4%

profile of v1, /device:TPU:0, one launch (start us, length us, event | category | flops | bytes accessed | tf_op | source)
XLA Modules:
  0.0 448.4 jit_solution(16060399996072132086)
XLA Ops:
  6.5 2.7 fusion.1
  9.2 0.0 all-gather.11.cloned.1.call-start
  9.3 0.7 all-gather.11.cloned.1.call-update
  10.0 0.0 all-gather.13.cloned.1.call-start
  10.0 0.7 all-gather.13.cloned.1.call-update
  10.7 0.0 all-gather.15.cloned.1.call-start
  10.8 0.5 all-gather.15.cloned.1.call-update
  11.3 0.0 reduce-scatter.11.cloned.1.call-start
  11.3 41.1 %all-gather.9.cloned.1.call-done = f32[2,1,1,96,2304]{4,3,0,2,1:T(8,128)} async-done(((f32[2,1,1,24,2304]{4,3,0,2,1:T(8,128)}), f32[2,1,1,96,2304]{4,3,0,2,1:T(8,128)}) %all-gather.9.cloned.1.call-update) | async-done | bytes 1769488 | tf_op jit(solution)/shard_map/all_gather | solution.py:259
  52.4 0.9 collective-permute-start
  53.3 39.9 %all-gather.11.cloned.1.call-done = f32[2,1,1,96,2304]{4,3,0,2,1:T(8,128)} async-done(((f32[2,1,1,24,2304]{4,3,0,2,1:T(8,128)}), f32[2,1,1,96,2304]{4,3,0,2,1:T(8,128)}) %all-gather.11.cloned.1.call-update) | async-done | bytes 1769488 | tf_op jit(solution)/shard_map/all_gather | solution.py:259
  93.2 0.9 collective-permute-start.1
  94.1 39.9 %all-gather.13.cloned.1.call-done = f32[2,1,1,96,2304]{4,3,0,2,1:T(8,128)} async-done(((f32[2,1,1,24,2304]{4,3,0,2,1:T(8,128)}), f32[2,1,1,96,2304]{4,3,0,2,1:T(8,128)}) %all-gather.13.cloned.1.call-update) | async-done | bytes 1769488 | tf_op jit(solution)/shard_map/all_gather | solution.py:259
  134.0 0.9 collective-permute-start.2
  134.9 39.8 %all-gather.15.cloned.1.call-done = f32[2,1,1,96,2304]{4,3,0,2,1:T(8,128)} async-done(((f32[2,1,1,24,2304]{4,3,0,2,1:T(8,128)}), f32[2,1,1,96,2304]{4,3,0,2,1:T(8,128)}) %all-gather.15.cloned.1.call-update) | async-done | bytes 1769488 | tf_op jit(solution)/shard_map/all_gather | solution.py:259
  174.6 0.9 collective-permute-start.3
  175.5 1.3 dynamic_slice.14
  179.4 1.3 dynamic_slice.12
  181.4 2.1 copy-done
  183.5 1.7 shard_map.118
  185.2 1.2 copy-done.5
  186.4 4.0 reshape.32
  190.4 0.9 copy-done.9
  191.3 0.9 copy-done.12
  192.2 2.7 shard_map.119
  194.9 3.0 reshape.33
  197.9 3.4 pad.13.refs_8_
  201.4 1.6 pad.14.refs_9_
  202.9 0.7 copy-done.3
  203.7 2.7 shard_map.120
  206.4 3.1 reshape.34
  209.4 3.4 pad.15.refs_10_
  212.8 2.7 shard_map.121
  215.5 3.1 reshape.35
  218.6 3.3 pad.16.refs_11_
  222.0 27.7 %shard_map.122 = (f32[2,96,24,128]{3,2,1,0:T(8,128)S(1)}, f32[2,96,24,128]{3,2,1,0:T(8,128)S(1)}, f32[2,96,24,128]{3,2,1,0:T(8,128)}, f32[2,96,24,128]{3,2,1,0:T(8,128)}) custom-call(f32[3]{0:T(128)S(1)} %fusion.shift_ref, bf16[192,192]{1,0:T(8,128)(2,1)S(1)} %copy-done.13, bf16[192,192]{1,0:T(8,128)(2,1)S(1)} %copy-done.10, bf16[192,192]{1,0:T(8,128)(2,1)S(1)} %copy-done.7, ...), custom_call_target="tpu_custom_call" | custom-call | tf_op jit(solution)/shard_map/pallas_call | solution.py:196
  249.7 1.4 copy-done.14
  251.1 0.7 copy-done.15
  251.8 2.1 reshape.39.pot_ref
  253.9 3.3 shard_map.126
  257.3 1.2 collective-permute-start.7
  258.5 20.8 %collective-permute-done.7 = f32[2,96,2304]{2,1,0:T(8,128)S(1)} collective-permute-done((f32[2,96,2304]{2,1,0:T(8,128)S(1)}, f32[2,96,2304]{2,1,0:T(8,128)S(1)}, u32[]{:S(2)}, u32[]{:S(2)}) %collective-permute-start.7) | collective-permute-done | bytes 1769504 | tf_op jit(solution)/shard_map/ppermute | solution.py:275
  279.3 1.4 add.60
  280.7 0.0 reduce-scatter.9.cloned.1.call-start
  280.7 2.1 reshape.38.pot_ref
  282.8 3.3 shard_map.125
  286.2 1.8 collective-permute-start.6
  288.0 20.2 %collective-permute-done.6 = f32[2,96,2304]{2,1,0:T(8,128)S(1)} collective-permute-done((f32[2,96,2304]{2,1,0:T(8,128)S(1)}, f32[2,96,2304]{2,1,0:T(8,128)S(1)}, u32[]{:S(2)}, u32[]{:S(2)}) %collective-permute-start.6) | collective-permute-done | bytes 1769504 | tf_op jit(solution)/shard_map/ppermute | solution.py:275
  308.2 1.4 add.59
  309.6 0.0 reduce-scatter.7.cloned.1.call-start
  309.6 2.1 reshape.37.pot_ref
  311.7 3.4 shard_map.124
  315.1 2.3 collective-permute-start.5
  317.4 20.0 %collective-permute-done.5 = f32[2,96,2304]{2,1,0:T(8,128)S(1)} collective-permute-done((f32[2,96,2304]{2,1,0:T(8,128)S(1)}, f32[2,96,2304]{2,1,0:T(8,128)S(1)}, u32[]{:S(2)}, u32[]{:S(2)}) %collective-permute-start.5) | collective-permute-done | bytes 1769504 | tf_op jit(solution)/shard_map/ppermute | solution.py:275
  337.5 1.4 add.58
  338.9 0.0 reduce-scatter.5.cloned.1.call-start
  339.0 2.1 reshape.36.pot_ref
  341.1 3.4 shard_map.123
  344.4 2.6 collective-permute-start.4
  347.0 20.0 %collective-permute-done.4 = f32[2,96,2304]{2,1,0:T(8,128)S(1)} collective-permute-done((f32[2,96,2304]{2,1,0:T(8,128)S(1)}, f32[2,96,2304]{2,1,0:T(8,128)S(1)}, u32[]{:S(2)}, u32[]{:S(2)}) %collective-permute-start.4) | collective-permute-done | bytes 1769504 | tf_op jit(solution)/shard_map/ppermute | solution.py:275
  367.0 1.5 add.57
  368.6 30.3 %reduce-scatter.7.cloned.1.call-done = f32[2,24,2304]{2,1,0:T(8,128)} async-done(((f32[2,96,2304]{2,1,0:T(8,128)}), f32[2,24,2304]{2,1,0:T(8,128)}) %reduce-scatter.7.cloned.1.call-update) | async-done | bytes 442384 | tf_op jit(solution)/shard_map/reduce_scatter | solution.py:278
  398.9 40.0 %reduce-scatter.5.cloned.1.call-done = f32[2,24,2304]{2,1,0:T(8,128)} async-done(((f32[2,96,2304]{2,1,0:T(8,128)}), f32[2,24,2304]{2,1,0:T(8,128)}) %reduce-scatter.5.cloned.1.call-update) | async-done | bytes 442384 | tf_op jit(solution)/shard_map/reduce_scatter | solution.py:278
  438.9 2.7 maximum_bitcast_fusion
  (51 shorter events, 0.2 us)
Async XLA Ops:
  6.5 45.9 %all-gather.9.cloned.1.call-start = ((), (), s32[]{:S(2)}) async-start(), calls=%async_computation.8 | async-start | bytes 2211840 | tf_op jit(solution)/shard_map/all_gather | solution.py:259
  9.2 172.1 %copy-start.21 = (s32[4,3]{1,0:T(4,128)S(1)}, s32[4,3]{1,0:T(4,128)}, u32[]{:S(2)}) copy-start(s32[4,3]{1,0:T(4,128)} %param.13) | copy-start | bytes 148
  9.2 172.2 %copy-start.8 = (bf16[192,192]{1,0:T(8,128)(2,1)S(1)}, bf16[192,192]{1,0:T(8,128)(2,1)}, u32[]{:S(2)}) copy-start(bf16[192,192]{1,0:T(8,128)(2,1)} %constant.77.clone.low_ref.refs_1_) | copy-start | bytes 221188
  9.2 172.2 %copy-start.11 = (bf16[192,192]{1,0:T(8,128)(2,1)S(1)}, bf16[192,192]{1,0:T(8,128)(2,1)}, u32[]{:S(2)}) copy-start(bf16[192,192]{1,0:T(8,128)(2,1)} %constant.76.clone.high_ref.refs_0_) | copy-start | bytes 221188
  9.2 84.0 %all-gather.11.cloned.1.call-start = ((), (), s32[]{:S(2)}) async-start(), calls=%async_computation.9 | async-start | bytes 2211840 | tf_op jit(solution)/shard_map/all_gather | solution.py:259
  10.0 124.0 %all-gather.13.cloned.1.call-start = ((), (), s32[]{:S(2)}) async-start(), calls=%async_computation.10 | async-start | bytes 2211840 | tf_op jit(solution)/shard_map/all_gather | solution.py:259
  10.7 163.9 %all-gather.15.cloned.1.call-start = ((), (), s32[]{:S(2)}) async-start(), calls=%async_computation.11 | async-start | bytes 2211840 | tf_op jit(solution)/shard_map/all_gather | solution.py:259
  11.3 357.3 %reduce-scatter.11.cloned.1.call-start = ((), (), s32[]{:S(2)}) async-start(), calls=%async_computation.7 | async-start | bytes 2211840 | tf_op jit(solution)/shard_map/reduce_scatter | solution.py:278
  52.4 129.0 %collective-permute-start = (f32[2,96,2304]{2,1,0:T(8,128)}, f32[2,96,2304]{2,1,0:T(8,128)S(1)}, u32[]{:S(2)}, u32[]{:S(2)}) collective-permute-start(f32[2,96,2304]{2,1,0:T(8,128)} %bitcast.26), channel_id=1, source_target_pairs={{16,0},{20,4},{4,8},{0,12},{28,16},{24,20},{8,24},{12,28},{25,1},{... | collective-permute-start | bytes 5308424 | tf_op jit(solution)/shard_map/ppermute | solution.py:260
  93.2 97.2 %collective-permute-start.1 = (f32[2,96,2304]{2,1,0:T(8,128)}, f32[2,96,2304]{2,1,0:T(8,128)}, u32[]{:S(2)}, u32[]{:S(2)}) collective-permute-start(f32[2,96,2304]{2,1,0:T(8,128)} %bitcast.29), channel_id=1, source_target_pairs={{16,0},{20,4},{4,8},{0,12},{28,16},{24,20},{8,24},{12,28},{25,1},{... | collective-permute-start | bytes 5308424 | tf_op jit(solution)/shard_map/ppermute | solution.py:260
  134.0 68.9 %collective-permute-start.2 = (f32[2,96,2304]{2,1,0:T(8,128)}, f32[2,96,2304]{2,1,0:T(8,128)}, u32[]{:S(2)}, u32[]{:S(2)}) collective-permute-start(f32[2,96,2304]{2,1,0:T(8,128)} %bitcast.32), channel_id=1, source_target_pairs={{16,0},{20,4},{4,8},{0,12},{28,16},{24,20},{8,24},{12,28},{25,1},{... | collective-permute-start | bytes 5308424 | tf_op jit(solution)/shard_map/ppermute | solution.py:260
  174.6 38.2 %collective-permute-start.3 = (f32[2,96,2304]{2,1,0:T(8,128)}, f32[2,96,2304]{2,1,0:T(8,128)}, u32[]{:S(2)}, u32[]{:S(2)}) collective-permute-start(f32[2,96,2304]{2,1,0:T(8,128)} %bitcast.35), channel_id=1, source_target_pairs={{16,0},{20,4},{4,8},{0,12},{28,16},{24,20},{8,24},{12,28},{25,1},{... | collective-permute-start | bytes 5308424 | tf_op jit(solution)/shard_map/ppermute | solution.py:260
  181.4 3.8 copy-start.2
  181.4 2.1 copy-start
  185.2 1.2 copy-start.5
  186.4 4.0 copy-start.1
  190.4 0.9 copy-start.9
  191.3 0.9 copy-start.12
  197.9 3.4 copy-start.20
  201.3 2.3 copy-start.3
  201.3 2.3 copy-start.10
  201.3 2.3 copy-start.13
  209.4 3.4 copy-start.4
  218.6 3.4 copy-start.6
  218.6 3.4 copy-start.7
  218.6 3.4 copy-start.16
  218.6 3.4 copy-start.17
  218.6 3.4 copy-start.18
  218.6 3.4 copy-start.19
  249.7 1.4 copy-start.14
  249.7 2.1 copy-start.15
  257.3 22.0 %collective-permute-start.7 = (f32[2,96,2304]{2,1,0:T(8,128)S(1)}, f32[2,96,2304]{2,1,0:T(8,128)S(1)}, u32[]{:S(2)}, u32[]{:S(2)}) collective-permute-start(f32[2,96,2304]{2,1,0:T(8,128)S(1)} %get-tuple-element.28), channel_id=1, source_target_pairs={{0,16},{4,20},{8,4},{12,0},{16,28},{20,24},{24,8},{28,12},{1,25},{... | collective-permute-start | bytes 5308424 | tf_op jit(solution)/shard_map/ppermute | solution.py:275
  280.7 88.0 %reduce-scatter.9.cloned.1.call-start = ((), (), s32[]{:S(2)}) async-start(), calls=%async_computation.6 | async-start | bytes 2211840 | tf_op jit(solution)/shard_map/reduce_scatter | solution.py:278
  286.2 22.0 %collective-permute-start.6 = (f32[2,96,2304]{2,1,0:T(8,128)S(1)}, f32[2,96,2304]{2,1,0:T(8,128)S(1)}, u32[]{:S(2)}, u32[]{:S(2)}) collective-permute-start(f32[2,96,2304]{2,1,0:T(8,128)S(1)} %get-tuple-element.25), channel_id=1, source_target_pairs={{0,16},{4,20},{8,4},{12,0},{16,28},{20,24},{24,8},{28,12},{1,25},{... | collective-permute-start | bytes 5308424 | tf_op jit(solution)/shard_map/ppermute | solution.py:275
  309.6 89.3 %reduce-scatter.7.cloned.1.call-start = ((), (), s32[]{:S(2)}) async-start(), calls=%async_computation.5 | async-start | bytes 2211840 | tf_op jit(solution)/shard_map/reduce_scatter | solution.py:278
  315.1 22.4 %collective-permute-start.5 = (f32[2,96,2304]{2,1,0:T(8,128)S(1)}, f32[2,96,2304]{2,1,0:T(8,128)S(1)}, u32[]{:S(2)}, u32[]{:S(2)}) collective-permute-start(f32[2,96,2304]{2,1,0:T(8,128)S(1)} %get-tuple-element.22), channel_id=1, source_target_pairs={{0,16},{4,20},{8,4},{12,0},{16,28},{20,24},{24,8},{28,12},{1,25},{... | collective-permute-start | bytes 5308424 | tf_op jit(solution)/shard_map/ppermute | solution.py:275
  338.9 99.9 %reduce-scatter.5.cloned.1.call-start = ((), (), s32[]{:S(2)}) async-start(), calls=%async_computation.4 | async-start | bytes 2211840 | tf_op jit(solution)/shard_map/reduce_scatter | solution.py:278
  344.4 22.6 %collective-permute-start.4 = (f32[2,96,2304]{2,1,0:T(8,128)S(1)}, f32[2,96,2304]{2,1,0:T(8,128)S(1)}, u32[]{:S(2)}, u32[]{:S(2)}) collective-permute-start(f32[2,96,2304]{2,1,0:T(8,128)S(1)} %get-tuple-element.19), channel_id=1, source_target_pairs={{0,16},{4,20},{8,4},{12,0},{16,28},{20,24},{24,8},{28,12},{1,25},{... | collective-permute-start | bytes 5308424 | tf_op jit(solution)/shard_map/ppermute | solution.py:275
Sparse Core Ops, SparseCore 0:
  9.3 43.0 all-gather.8
  54.0 39.1 all-gather.10
  94.8 39.1 all-gather.12
  135.4 39.1 all-gather.14
  280.8 38.4 reduce-scatter.10
  321.5 37.4 reduce-scatter.8
  361.4 37.4 reduce-scatter.6
  401.3 37.4 reduce-scatter.4

commit v2 on v1

--- a/solution.py
+++ b/solution.py
@@ -13,7 +13,8 @@
 SCREENING = 0.5
 CHUNKS = 4
 LANES = 128
-VMEM = 48 * 1024 * 1024
+VMEM = 56 * 1024 * 1024
+MESH = pl.DeviceIdType.MESH
 
 
 def splits(table):
@@ -89,11 +90,11 @@
     left, left_inverse, right, right_inverse = [
         (tables_refs[2 * i][...], tables_refs[2 * i + 1][...]) for i in range(4)
     ]
-    count = len(refs) // 2
-    ins, outs = refs[:count], refs[count:]
-    planes, part, padded = ins[0].shape[1:]
+    ins, outs = refs
+    count, _, planes, part, padded = ins.shape
     columns = [
-        jnp.concatenate([r[c, i] for c in range(2) for r in ins], axis=0) for i in range(planes)
+        jnp.concatenate([ins[j, c, i] for c in range(2) for j in range(count)], axis=0)
+        for i in range(planes)
     ]
     field = product(left, halves(jnp.concatenate(columns, axis=1)))
 
@@ -149,9 +150,9 @@
     field = product(left_inverse, halves(jnp.concatenate(columns, axis=1)))
     for c in range(2):
         for i in range(planes):
-            for j, out in enumerate(outs):
+            for j in range(count):
                 start = c * grid + j * part
-                out[c, i] = field[start : start + part, i * padded : (i + 1) * padded]
+                outs[j, c, i] = field[start : start + part, i * padded : (i + 1) * padded]
 
 
 def whole(array):
@@ -191,8 +192,8 @@
 def filtered(parts, shift, all_tables, grid, scale):
     planes = next(p for p in (8, 6, 4, 3, 2, 1) if grid % p == 0)
     flat = [t for pair in all_tables for t in pair]
-    block = (2, planes) + parts[0].shape[2:]
-    spec = pl.BlockSpec(block, lambda i: (0, i, 0, 0))
+    block = parts[0].shape[:2] + (planes,) + parts[0].shape[3:]
+    spec = pl.BlockSpec(block, lambda i: (0, 0, i, 0, 0))
     return pl.pallas_call(
         functools.partial(filter_kernel, grid, scale),
         grid=(grid // planes,),
@@ -201,6 +202,373 @@
         out_shape=[jax.ShapeDtypeStruct(p.shape, jnp.float32) for p in parts],
         compiler_params=pltpu.CompilerParams(vmem_limit_bytes=VMEM),
     )(shift, *flat, *parts)
+
+
+def position():
+    kpair, band, pencil = (lax.axis_index(a) for a in ("kpair", "band", "pencil"))
+    x, core = kpair // 2, kpair % 2
+    high, low = pencil // 2, pencil % 2
+    side = (core + x * (1 - low) + band * low * (1 - high)) % 2
+
+    def partner(side):
+        flip_x = 1 - side
+        flip_y = high + side * (1 - 2 * high)
+        flip_core = low + side * (high + (1 - high) * (1 - low) - low)
+        return {
+            "kpair": (x + flip_x) % 2 * 2 + (core + flip_core) % 2,
+            "band": (band + flip_y) % 2,
+        }
+
+    return pencil, partner(side), partner(1 - side)
+
+
+def greet(pencil, pencils, sender, receiver):
+    barrier = pltpu.get_barrier_semaphore()
+    for step in (-1, 1):
+
+        @pl.when((pencil + step >= 0) & (pencil + step < pencils))
+        def _():
+            pl.semaphore_signal(
+                barrier, inc=1, device_id={"pencil": pencil + step}, device_id_type=MESH
+            )
+
+    pl.semaphore_signal(barrier, inc=1, device_id=sender, device_id_type=MESH)
+    inner = ((pencil > 0) & (pencil < pencils - 1)).astype(jnp.int32)
+    pl.semaphore_wait(barrier, 2 + inner)
+
+
+def stacked(ref, chunk, component, pencils, columns):
+    return jnp.concatenate([ref[chunk, q, component, :, columns] for q in range(pencils)], axis=0)
+
+
+def gather_kernel(
+    pencils,
+    flag_ref,
+    high_ref,
+    low_ref,
+    source,
+    own_out,
+    far_out,
+    spectrum_out,
+    own,
+    far,
+    spectrum,
+    load_sem,
+    z_send,
+    z_recv,
+    f_send,
+    f_recv,
+    own_sem,
+    far_sem,
+    out_sem,
+):
+    chunks, _, _, slab, lanes = own.shape
+    grid = pencils * slab
+    pencil, fetch, give = position()
+    loads = [
+        pltpu.make_async_copy(
+            source.at[:, :, pl.ds(j * lanes, lanes)], own.at[j, pencil], load_sem.at[j]
+        )
+        for j in range(chunks)
+    ]
+    for load in loads:
+        load.start()
+    greet(pencil, pencils, fetch, give)
+
+    def line(way, hop, j, q, step=None):
+        step = 1 - 2 * way if step is None else step
+        return pltpu.make_async_remote_copy(
+            own.at[j, q],
+            own.at[j, q],
+            z_send.at[way, hop, j],
+            z_recv.at[way, hop, j],
+            device_id={"pencil": pencil + step},
+            device_id_type=MESH,
+        )
+
+    def across(j, q):
+        return pltpu.make_async_remote_copy(
+            own.at[j, q],
+            far.at[j, q],
+            f_send.at[q, j],
+            f_recv.at[q, j],
+            device_id=give,
+            device_id_type=MESH,
+        )
+
+    def sends(way, hop):
+        if way == 0:
+            return (pencil < pencils - 1) & (pencil >= hop)
+        return (pencil > 0) & (pencil + hop < pencils)
+
+    def receives(way, hop):
+        return pencil >= hop + 1 if way == 0 else pencil + hop + 1 < pencils
+
+    block = lane_block(lanes)
+
+    def compute(j):
+        for q in range(pencils):
+            across(j, q).wait_recv()
+        pltpu.make_async_copy(own.at[j], own_out.at[j], own_sem.at[j]).start()
+        pltpu.make_async_copy(far.at[j], far_out.at[j], far_sem.at[j]).start()
+        packed = flag_ref[0] > 0
+        for b in range(lanes // block):
+            columns = pl.ds(b * block, block)
+            gr, gi = (stacked(own, j, c, pencils, columns) for c in range(2))
+            hr, hi = (stacked(far, j, c, pencils, columns) for c in range(2))
+            real = jnp.where(packed, gr * gr + gi * gi, hr * gr + hi * gi)
+            imag = jnp.where(packed, hr * hr + hi * hi, hr * gi - hi * gr)
+            result = product(
+                (high_ref[...], low_ref[...]), halves(jnp.concatenate([real, imag], axis=0))
+            )
+            spectrum[j, 0, :, columns] = result[:grid]
+            spectrum[j, 1, :, columns] = result[grid:]
+        pltpu.make_async_copy(spectrum.at[j], spectrum_out.at[j], out_sem.at[j]).start()
+
+    for j in range(chunks):
+        loads[j].wait()
+        for way in range(2):
+
+            @pl.when(sends(way, 0))
+            def _():
+                line(way, 0, j, pencil).start()
+
+        across(j, pencil).start()
+    for hop in range(pencils - 1):
+        for j in range(chunks):
+            for way in range(2):
+
+                @pl.when(receives(way, hop))
+                def _():
+                    q = pencil - (1 - 2 * way) * (hop + 1)
+                    line(way, hop, j, q, 2 * way - 1).wait_recv()
+                    if hop < pencils - 2:
+
+                        @pl.when(sends(way, hop + 1))
+                        def _():
+                            line(way, hop + 1, j, q).start()
+
+                    across(j, q).start()
+
+            if hop == pencils - 2 and j > 0:
+                compute(j - 1)
+    compute(chunks - 1)
+    for j in range(chunks):
+        for hop in range(pencils - 1):
+            for way in range(2):
+
+                @pl.when(sends(way, hop))
+                def _():
+                    line(way, hop, j, pencil - (1 - 2 * way) * hop).wait_send()
+
+        for q in range(pencils):
+            across(j, q).wait_send()
+        pltpu.make_async_copy(own.at[j], own_out.at[j], own_sem.at[j]).wait()
+        pltpu.make_async_copy(far.at[j], far_out.at[j], far_sem.at[j]).wait()
+        pltpu.make_async_copy(spectrum.at[j], spectrum_out.at[j], out_sem.at[j]).wait()
+
+
+def scatter_kernel(
+    pencils,
+    flag_ref,
+    high_ref,
+    low_ref,
+    pot_in,
+    own_in,
+    far_in,
+    out,
+    pot,
+    own,
+    far,
+    back,
+    arrived,
+    load_sem,
+    r_send,
+    r_recv,
+    z_send,
+    z_recv,
+    out_sem,
+):
+    chunks, _, _, slab, lanes = own.shape
+    grid = pencils * slab
+    pencil, fetch, give = position()
+
+    def loads(j):
+        return [
+            pltpu.make_async_copy(a.at[j], b.at[j], load_sem.at[i, j])
+            for i, (a, b) in enumerate(((pot_in, pot), (own_in, own), (far_in, far)))
+        ]
+
+    for j in range(chunks):
+        for load in loads(j):
+            load.start()
+    greet(pencil, pencils, give, fetch)
+
+    def across(j):
+        return pltpu.make_async_remote_copy(
+            far.at[j],
+            back.at[j],
+            r_send.at[j],
+            r_recv.at[j],
+            device_id=fetch,
+            device_id_type=MESH,
+        )
+
+    def line(way, left, j):
+        step = 1 - 2 * way
+        return pltpu.make_async_remote_copy(
+            own.at[j, pencil + step * (left + 1)],
+            arrived.at[j, way, left],
+            z_send.at[way, left, j],
+            z_recv.at[way, left, j],
+            device_id={"pencil": pencil + step},
+            device_id_type=MESH,
+        )
+
+    def landing(way, left, j):
+        return pltpu.make_async_remote_copy(
+            own.at[j, pencil],
+            arrived.at[j, way, left],
+            z_send.at[way, left, j],
+            z_recv.at[way, left, j],
+            device_id={"pencil": pencil - 1 + 2 * way},
+            device_id_type=MESH,
+        )
+
+    def sends(way, left):
+        return pencil + left + 1 < pencils if way == 0 else pencil - left - 1 >= 0
+
+    def has_previous(way):
+        return pencil > 0 if way == 0 else pencil < pencils - 1
+
+    block = lane_block(lanes)
+
+    def compute(j):
+        for load in loads(j):
+            load.wait()
+        packed = flag_ref[0] > 0
+        for b in range(lanes // block):
+            columns = pl.ds(b * block, block)
+            field = product(
+                (high_ref[...], low_ref[...]),
+                halves(jnp.concatenate([pot[j, 0, :, columns], pot[j, 1, :, columns]], axis=0)),
+            )
+            for q in range(pencils):
+                vr = field[q * slab : (q + 1) * slab]
+                vi = field[grid + q * slab : grid + (q + 1) * slab]
+                gr, gi = own[j, q, 0, :, columns], own[j, q, 1, :, columns]
+                hr, hi = far[j, q, 0, :, columns], far[j, q, 1, :, columns]
+                own[j, q, 0, :, columns] = jnp.where(packed, gr * vr, hr * vr - hi * vi)
+                own[j, q, 1, :, columns] = jnp.where(packed, gi * vr, hr * vi + hi * vr)
+                far[j, q, 0, :, columns] = jnp.where(packed, hr * vi, gr * vr + gi * vi)
+                far[j, q, 1, :, columns] = jnp.where(packed, hi * vi, gi * vr - gr * vi)
+        across(j).start()
+
+    def finish(j):
+        for way in range(2):
+
+            @pl.when(has_previous(way))
+            def _():
+                landing(way, 0, j).wait_recv()
+                own[j, pencil] = own[j, pencil] + arrived[j, way, 0]
+
+        pltpu.make_async_copy(
+            own.at[j, pencil], out.at[:, :, pl.ds(j * lanes, lanes)], out_sem.at[j]
+        ).start()
+
+    for j in range(chunks):
+        compute(j)
+    for j in range(chunks):
+        across(j).wait_recv()
+        for q in range(pencils):
+            own[j, q] = own[j, q] + back[j, q]
+        for left in range(pencils - 2, -1, -1):
+            for way in range(2):
+
+                @pl.when(sends(way, left))
+                def _():
+                    if left + 1 < pencils - 1:
+
+                        @pl.when(has_previous(way))
+                        def _():
+                            landing(way, left + 1, j).wait_recv()
+                            q = pencil + (1 - 2 * way) * (left + 1)
+                            own[j, q] = own[j, q] + arrived[j, way, left + 1]
+
+                    line(way, left, j).start()
+
+        if j > 0:
+            finish(j - 1)
+    finish(chunks - 1)
+    for j in range(chunks):
+        across(j).wait_send()
+        for left in range(pencils - 1):
+            for way in range(2):
+
+                @pl.when(sends(way, left))
+                def _():
+                    line(way, left, j).wait_send()
+
+        pltpu.make_async_copy(
+            own.at[j, pencil], out.at[:, :, pl.ds(j * lanes, lanes)], out_sem.at[j]
+        ).wait()
+
+
+ANY = pl.BlockSpec(memory_space=pl.ANY)
+WHOLE = pl.BlockSpec(memory_space=pltpu.VMEM)
+
+
+def gathered(piece, flag, table, pencils):
+    _, slab, plane = piece.shape
+    grid, lanes = slab * pencils, plane // CHUNKS
+    fields = (CHUNKS, pencils, 2, slab, lanes)
+    spectrum = (CHUNKS, 2, grid, lanes)
+    dma = pltpu.SemaphoreType.DMA
+    return pl.pallas_call(
+        functools.partial(gather_kernel, pencils),
+        in_specs=[SCALARS, WHOLE, WHOLE, ANY],
+        out_specs=[ANY] * 3,
+        out_shape=[jax.ShapeDtypeStruct(s, jnp.float32) for s in (fields, fields, spectrum)],
+        scratch_shapes=[pltpu.VMEM(s, jnp.float32) for s in (fields, fields, spectrum)]
+        + [
+            dma((CHUNKS,)),
+            dma((2, pencils - 1, CHUNKS)),
+            dma((2, pencils - 1, CHUNKS)),
+            dma((pencils, CHUNKS)),
+            dma((pencils, CHUNKS)),
+            dma((CHUNKS,)),
+            dma((CHUNKS,)),
+            dma((CHUNKS,)),
+        ],
+        compiler_params=pltpu.CompilerParams(
+            collective_id=0, has_side_effects=True, vmem_limit_bytes=VMEM
+        ),
+    )(flag, *table, piece)
+
+
+def scattered(potential, own, far, flag, table, pencils):
+    _, _, _, slab, lanes = own.shape
+    dma = pltpu.SemaphoreType.DMA
+    arrived = (CHUNKS, 2, pencils - 1, 2, slab, lanes)
+    shapes = (potential.shape, own.shape, own.shape, own.shape, arrived)
+    return pl.pallas_call(
+        functools.partial(scatter_kernel, pencils),
+        in_specs=[SCALARS, WHOLE, WHOLE] + [ANY] * 3,
+        out_specs=ANY,
+        out_shape=jax.ShapeDtypeStruct((2, slab, lanes * CHUNKS), jnp.float32),
+        scratch_shapes=[pltpu.VMEM(s, jnp.float32) for s in shapes]
+        + [
+            dma((3, CHUNKS)),
+            dma((CHUNKS,)),
+            dma((CHUNKS,)),
+            dma((2, pencils - 1, CHUNKS)),
+            dma((2, pencils - 1, CHUNKS)),
+            dma((CHUNKS,)),
+        ],
+        compiler_params=pltpu.CompilerParams(
+            collective_id=1, has_side_effects=True, vmem_limit_bytes=VMEM
+        ),
+    )(flag, *table, potential, own, far)
 
 
 def schedule(kpts, bands, sets):
@@ -253,6 +621,17 @@
     lanes = plane // CHUNKS
     part = lanes // grid
 
+    scale = -1.0 / (count * grid**3)
+
+    if pencils == 4 and slab % 8 == 0:
+        own, other, spectrum = gathered(orbitals[:, 0, 0], flag, all_tables[0], pencils)
+        spectrum = spectrum.reshape(CHUNKS, 2, grid, part, grid)
+        spectrum = jnp.pad(spectrum, ((0, 0),) * 4 + ((0, padded - grid),))
+        potential = filtered([spectrum], shift, all_tables, grid, scale)[0]
+        potential = potential[..., :grid].reshape(CHUNKS, 2, grid, lanes)
+        result = scattered(potential, own, other, flag, all_tables[1], pencils)
+        return result[:, None, None]
+
     own_chunks, far_chunks, spectra = [], [], []
     for j in range(CHUNKS):
         piece = orbitals[:, 0, 0, :, j * lanes : (j + 1) * lanes]
@@ -264,8 +643,7 @@
         spectrum = spectrum.reshape(2, grid, part, grid)
         spectra.append(jnp.pad(spectrum, ((0, 0), (0, 0), (0, 0), (0, padded - grid))))
 
-    scale = -1.0 / (count * grid**3)
-    potentials = filtered(spectra, shift, all_tables, grid, scale)
+    potentials = filtered([jnp.stack(spectra)], shift, all_tables, grid, scale)[0]
     results = []
     for j in range(CHUNKS):
         potential = potentials[j][..., :grid].reshape(2, grid, lanes)

time: 449 us -> 340 us (0.76)
  waiting for transfers between devices: 314 us -> 0 us
  Pallas kernels: 50.8 us -> 300 us
  between operations: 17.1 us -> 2.94 us
  local copies, waits for them, and re-layouts: 46.3 us -> 34.3 us
  starting transfers between devices: 11.7 us -> 0 us
  other arithmetic: 8.45 us -> 1.22 us
    pallas_call x8 -> x2, Pallas kernels: 23.1 us -> 273 us  [the longest x1 142 us: scattered(): pl.pallas_call(functools.partial(scatter_kernel, pencils), in_specs=[SCAL...]
    all_gather x4 -> x0, waiting for transfers between devices: 161 us -> none  [body(): own = lax.all_gather(piece, 'pencil', axis=1, tiled=True)]
    ppermute x8 -> x0, waiting for transfers between devices: 81.1 us -> none  [the longest x4 81.1 us: body(): total = direct + lax.ppermute(reverse, axes, give)]
    reduce_scatter x4 -> x0, waiting for transfers between devices: 70.3 us -> none  [body(): lax.psum_scatter(total, 'pencil', scatter_dimension=1, tiled=True)]
    ppermute x8 -> x0, starting transfers between devices: 11.4 us -> none  [the longest x4 7.92 us: body(): total = direct + lax.ppermute(reverse, axes, give)]
    add x4 -> x0, other arithmetic: 5.7 us -> none  [body(): total = direct + lax.ppermute(reverse, axes, give)]
    unnamed x44 -> x1, local copies, waits for them, and re-layouts: 8 us -> 2.8 us
    pad x4 -> x1, local copies, waits for them, and re-layouts: 11.7 us -> 7.92 us  [body(): spectrum = jnp.pad(spectrum, ((0, 0),) * 4 + ((0, padded - grid),))]
  transfers between devices with their start and end apart: 16 -> 0, of which waited for: 10 -> 0; matrix products, arithmetic and copies ran while one was open for 7% -> 0% of each run, Pallas kernels for 4% -> 0%
where the time goes in v2:
time: 340 us; the launch traced here: 339 us
  Pallas kernels  300 us (88%)
  local copies, waits for them, and re-layouts  34.3 us (10%)
    pallas_call x1, Pallas kernels, scattered(): pl.pallas_call(functools.partial(scatter_kernel, pencils), in_specs=[SCAL...  142 us
    pallas_call x1, Pallas kernels, gathered(): pl.pallas_call(functools.partial(gather_kernel, pencils), in_specs=[SCALA...  131 us
    pallas_call x1, Pallas kernels, filtered(): pl.pallas_call(functools.partial(filter_kernel, grid, scale), grid=(grid...  27.4 us
    reshape x1, local copies, waits for them, and re-layouts, body(): spectrum = spectrum.reshape(CHUNKS, 2, grid, part, grid)  11.1 us
    reshape x1, local copies, waits for them, and re-layouts, body(): potential = potential[..., :grid].reshape(CHUNKS, 2, grid, lanes)  10 us
    pad x1, local copies, waits for them, and re-layouts, body(): spectrum = jnp.pad(spectrum, ((0, 0),) * 4 + ((0, padded - grid),))  7.92 us

profile of v2, /device:TPU:0, one launch (start us, length us, event | category | flops | bytes accessed | tf_op | source)
XLA Modules:
  0.0 338.8 jit_solution(8787331798683350664)
XLA Ops:
  0.0 1.3 dynamic_slice.12
  1.9 1.3 dynamic_slice.14
  5.4 0.7 convert_multiply_fusion
  6.1 0.5 fusion.shift_ref
  6.7 130.8 %shard_map.118 = (f32[4,4,2,24,2304]{4,3,2,1,0:T(8,128)}, f32[4,4,2,24,2304]{4,3,2,1,0:T(8,128)}, f32[4,2,96,2304]{3,2,1,0:T(8,128)}) custom-call(s32[1]{0:T(128)} %bitcast.1.flag_ref, bf16[192,192]{1,0:T(8,128)(2,1)} %constant.76.clone.high_ref.refs_0_, bf16[192,192]{1,0:T(8,128)(2,1)} %constant.77.clone.low_ref.refs_1_, f32[2,24,9216]{2,1,0:T(8,128)} %bitcast.16), custom_call_target="tpu_custom_call" | custom-call | tf_op jit(solution)/shard_map/pallas_call | solution.py:527
  137.5 11.1 %reshape.14 = f32[4,2,96,24,96]{4,3,2,1,0:T(8,128)} reshape(f32[4,2,96,2304]{3,2,1,0:T(8,128)} %get-tuple-element.8) | data formatting | bytes 14155776 | tf_op jit(solution)/shard_map/reshape | solution.py:628
  148.6 7.9 %pad.4.refs_8_ = f32[4,2,96,24,128]{4,3,2,1,0:T(8,128)} pad(f32[4,2,96,24,96]{4,3,2,1,0:T(8,128)} %reshape.14, f32[]{:T(128)} %constant.70.clone.1), padding=0_0x0_0x0_0x0_0x0_32 | pad | bytes 16515076 | tf_op jit(solution)/shard_map/jit(_pad)/pad | solution.py:629
  156.5 27.4 %shard_map.119 = f32[4,2,96,24,128]{4,3,2,1,0:T(8,128)} custom-call(f32[3]{0:T(128)} %fusion.shift_ref, bf16[192,192]{1,0:T(8,128)(2,1)} %constant.76.clone.high_ref.refs_0_, bf16[192,192]{1,0:T(8,128)(2,1)} %constant.77.clone.low_ref.refs_1_, bf16[192,192]{1,0:T(8,128)(2,1)} %constant.78.clone.refs_2_.high_ref, ...), custom_call_target="tpu_custom_call" | custom-call | tf_op jit(solution)/shard_map/pallas_call | solution.py:197
  183.9 10.0 %reshape.15.pot_in = f32[4,2,96,2304]{3,2,1,0:T(8,128)} reshape(f32[4,2,96,24,96]{4,3,2,1,0:T(8,128)} %bitcast.14) | data formatting | bytes 14155776 | tf_op jit(solution)/shard_map/reshape | solution.py:631
  193.9 142.1 %shard_map.120 = f32[2,24,9216]{2,1,0:T(8,128)} custom-call(s32[1]{0:T(128)} %bitcast.1.flag_ref, bf16[192,192]{1,0:T(8,128)(2,1)} %constant.78.clone.refs_2_.high_ref, bf16[192,192]{1,0:T(8,128)(2,1)} %constant.79.clone.refs_3_.low_ref, f32[4,2,96,2304]{3,2,1,0:T(8,128)} %reshape.15.pot_in, f32[4,4,2,24,2304]{4,3,2,1,0:T(8,128)} %get-tuple-element.9.own_in, ...), custom_call_target="tpu_custom_call" | custom-call | tf_op jit(solution)/shard_map/pallas_call | solution.py:554
  336.0 2.8 copy.15

commit v3 on v2

--- a/solution.py
+++ b/solution.py
@@ -11,7 +11,7 @@
 from jax.sharding import PartitionSpec as P
 
 SCREENING = 0.5
-CHUNKS = 4
+CHUNKS = 6
 LANES = 128
 VMEM = 56 * 1024 * 1024
 MESH = pl.DeviceIdType.MESH
@@ -85,6 +85,16 @@
     reverse_ref[1] = jnp.where(packed, hi * vi, gi * vr - gr * vi)
 
 
+def offset_of(coords_ref):
+    _, fetch, _, diagonal = position()
+    own, far = lax.axis_index("kpair"), fetch["kpair"]
+    return [
+        (coords_ref[own, a] - coords_ref[far, a]).astype(jnp.float32)
+        * (0.25 * (1 - diagonal).astype(jnp.float32))
+        for a in range(3)
+    ]
+
+
 def filter_kernel(grid, scale, shift_ref, *refs):
     tables_refs, refs = refs[:8], refs[8:]
     left, left_inverse, right, right_inverse = [
@@ -118,14 +128,15 @@
     def frequency(index):
         return jnp.where(index < grid // 2, index, index - grid).astype(jnp.float32)
 
+    shift = [shift_ref[a] for a in range(3)] if len(shift_ref.shape) == 1 else offset_of(shift_ref)
     first = pl.program_id(0) * planes
-    ky = frequency(lax.broadcasted_iota(jnp.int32, (grid, padded), 0)) + shift_ref[1]
-    kz = frequency(lax.broadcasted_iota(jnp.int32, (grid, padded), 1)) + shift_ref[2]
+    ky = frequency(lax.broadcasted_iota(jnp.int32, (grid, padded), 0)) + shift[1]
+    kz = frequency(lax.broadcasted_iota(jnp.int32, (grid, padded), 1)) + shift[2]
     radius = grid // 2 - 1
     factor = (2.0 * math.pi / grid) ** 2
     filters = []
     for i in range(planes):
-        kx = frequency(jnp.full((grid, padded), first + i, jnp.int32)) + shift_ref[0]
+        kx = frequency(jnp.full((grid, padded), first + i, jnp.int32)) + shift[0]
         squared = kx * kx + ky * ky + kz * kz
         filters.append(
             jnp.where(
@@ -167,6 +178,12 @@
         if lanes % parts == 0 and lanes // parts % LANES == 0 and lanes // parts <= 1280:
             return lanes // parts
     return lanes
+
+
+def row_block(lanes, grid):
+    step = math.lcm(grid, LANES)
+    fits = [b for b in range(step, 1281, step) if lanes % b == 0]
+    return fits[-1] if fits else lanes
 
 
 def along_x(kernel, results, flag, table, *fields):
@@ -219,7 +236,7 @@
             "band": (band + flip_y) % 2,
         }
 
-    return pencil, partner(side), partner(1 - side)
+    return pencil, partner(side), partner(1 - side), side * high * low
 
 
 def greet(pencil, pencils, sender, receiver):
@@ -237,13 +254,45 @@
     pl.semaphore_wait(barrier, 2 + inner)
 
 
+def tile_roll(tile, amount):
+    return pltpu.roll(tile, amount % LANES, 1)
+
+
+def unflatten(flat, grid):
+    rows = flat.shape[1] // grid
+    tiles = [flat[:, t : t + LANES] for t in range(0, flat.shape[1], LANES)]
+    lane = lax.broadcasted_iota(jnp.int32, tiles[0].shape, 1)
+    result = []
+    for y in range(rows):
+        tile, offset = divmod(y * grid, LANES)
+        value = tile_roll(tiles[tile], -offset) if offset else tiles[tile]
+        if offset + grid > LANES:
+            after = tile_roll(tiles[tile + 1], -offset)
+            value = jnp.where(lane < LANES - offset, value, after)
+        result.append(value)
+    return result
+
+
+def flatten(rows, grid):
+    total = len(rows) * grid
+    lane = lax.broadcasted_iota(jnp.int32, rows[0].shape, 1)
+    rolled = [tile_roll(r, y * grid) if y * grid % LANES else r for y, r in enumerate(rows)]
+    tiles = []
+    for start in range(0, total, LANES):
+        first, last = start // grid, (start + LANES - 1) // grid
+        value = rolled[first]
+        for y in range(first + 1, last + 1):
+            value = jnp.where(lane < y * grid - start, value, rolled[y])
+        tiles.append(value)
+    return jnp.concatenate(tiles, axis=1)
+
+
 def stacked(ref, chunk, component, pencils, columns):
     return jnp.concatenate([ref[chunk, q, component, :, columns] for q in range(pencils)], axis=0)
 
 
 def gather_kernel(
     pencils,
-    flag_ref,
     high_ref,
     low_ref,
     source,
@@ -264,7 +313,7 @@
 ):
     chunks, _, _, slab, lanes = own.shape
     grid = pencils * slab
-    pencil, fetch, give = position()
+    pencil, fetch, give, diagonal = position()
     loads = [
         pltpu.make_async_copy(
             source.at[:, :, pl.ds(j * lanes, lanes)], own.at[j, pencil], load_sem.at[j]
@@ -304,14 +353,21 @@
     def receives(way, hop):
         return pencil >= hop + 1 if way == 0 else pencil + hop + 1 < pencils
 
-    block = lane_block(lanes)
+    block = row_block(lanes, grid)
+    part = lanes // grid
+
+    def publish(j):
+        rows = pl.ds(j * part, part)
+        return pltpu.make_async_copy(
+            spectrum.at[:, :, rows, :], spectrum_out.at[:, :, rows, :], out_sem.at[j]
+        )
 
     def compute(j):
         for q in range(pencils):
             across(j, q).wait_recv()
         pltpu.make_async_copy(own.at[j], own_out.at[j], own_sem.at[j]).start()
         pltpu.make_async_copy(far.at[j], far_out.at[j], far_sem.at[j]).start()
-        packed = flag_ref[0] > 0
+        packed = diagonal > 0
         for b in range(lanes // block):
             columns = pl.ds(b * block, block)
             gr, gi = (stacked(own, j, c, pencils, columns) for c in range(2))
@@ -321,9 +377,11 @@
             result = product(
                 (high_ref[...], low_ref[...]), halves(jnp.concatenate([real, imag], axis=0))
             )
-            spectrum[j, 0, :, columns] = result[:grid]
-            spectrum[j, 1, :, columns] = result[grid:]
-        pltpu.make_async_copy(spectrum.at[j], spectrum_out.at[j], out_sem.at[j]).start()
+            for m, value in enumerate(unflatten(result, grid)):
+                y = (j * lanes + b * block) // grid + m
+                spectrum[0, :, y, :] = value[:grid]
+                spectrum[1, :, y, :] = value[grid:]
+        publish(j).start()
 
     for j in range(chunks):
         loads[j].wait()
@@ -365,12 +423,11 @@
             across(j, q).wait_send()
         pltpu.make_async_copy(own.at[j], own_out.at[j], own_sem.at[j]).wait()
         pltpu.make_async_copy(far.at[j], far_out.at[j], far_sem.at[j]).wait()
-        pltpu.make_async_copy(spectrum.at[j], spectrum_out.at[j], out_sem.at[j]).wait()
+        publish(j).wait()
 
 
 def scatter_kernel(
     pencils,
-    flag_ref,
     high_ref,
     low_ref,
     pot_in,
@@ -391,12 +448,16 @@
 ):
     chunks, _, _, slab, lanes = own.shape
     grid = pencils * slab
-    pencil, fetch, give = position()
+    pencil, fetch, give, diagonal = position()
+
+    part = lanes // grid
 
     def loads(j):
+        rows = pl.ds(j * part, part)
+        pairs = [(pot_in.at[:, :, rows, :], pot.at[:, :, rows, :])]
+        pairs += [(a.at[j], b.at[j]) for a, b in ((own_in, own), (far_in, far))]
         return [
-            pltpu.make_async_copy(a.at[j], b.at[j], load_sem.at[i, j])
-            for i, (a, b) in enumerate(((pot_in, pot), (own_in, own), (far_in, far)))
+            pltpu.make_async_copy(a, b, load_sem.at[i, j]) for i, (a, b) in enumerate(pairs)
         ]
 
     for j in range(chunks):
@@ -404,12 +465,17 @@
             load.start()
     greet(pencil, pencils, give, fetch)
 
-    def across(j):
+    upper = pencil // (pencils // 2)
+
+    def across(j, i):
+        return back_of(j, upper * i + (1 - upper) * (pencils - 1 - i))
+
+    def back_of(j, q):
         return pltpu.make_async_remote_copy(
-            far.at[j],
-            back.at[j],
-            r_send.at[j],
-            r_recv.at[j],
+            far.at[j, q],
+            back.at[j, q],
+            r_send.at[q, j],
+            r_recv.at[q, j],
             device_id=fetch,
             device_id_type=MESH,
         )
@@ -441,17 +507,22 @@
     def has_previous(way):
         return pencil > 0 if way == 0 else pencil < pencils - 1
 
-    block = lane_block(lanes)
+    block = row_block(lanes, grid)
 
     def compute(j):
         for load in loads(j):
             load.wait()
-        packed = flag_ref[0] > 0
+        packed = diagonal > 0
         for b in range(lanes // block):
             columns = pl.ds(b * block, block)
+            first = (j * lanes + b * block) // grid
+            rows = [
+                jnp.concatenate([pot[0, :, y, :], pot[1, :, y, :]], axis=0)
+                for y in range(first, first + block // grid)
+            ]
             field = product(
                 (high_ref[...], low_ref[...]),
-                halves(jnp.concatenate([pot[j, 0, :, columns], pot[j, 1, :, columns]], axis=0)),
+                halves(flatten(rows, grid)),
             )
             for q in range(pencils):
                 vr = field[q * slab : (q + 1) * slab]
@@ -462,9 +533,20 @@
                 own[j, q, 1, :, columns] = jnp.where(packed, gi * vr, hr * vi + hi * vr)
                 far[j, q, 0, :, columns] = jnp.where(packed, hr * vi, gr * vr + gi * vi)
                 far[j, q, 1, :, columns] = jnp.where(packed, hi * vi, gi * vr - gr * vi)
-        across(j).start()
+        for i in range(pencils):
+            across(j, i).start()
+
+    def merge(j, left, way):
+        q = pencil + (1 - 2 * way) * (left + 1)
+        back_of(j, q).wait_recv()
+        own[j, q] = own[j, q] + back[j, q]
+
+    def merge_own(j):
+        back_of(j, pencil).wait_recv()
+        own[j, pencil] = own[j, pencil] + back[j, pencil]
 
     def finish(j):
+        merge_own(j)
         for way in range(2):
 
             @pl.when(has_previous(way))
@@ -476,17 +558,16 @@
             own.at[j, pencil], out.at[:, :, pl.ds(j * lanes, lanes)], out_sem.at[j]
         ).start()
 
+    compute(0)
     for j in range(chunks):
-        compute(j)
-    for j in range(chunks):
-        across(j).wait_recv()
-        for q in range(pencils):
-            own[j, q] = own[j, q] + back[j, q]
+        if j + 1 < chunks:
+            compute(j + 1)
         for left in range(pencils - 2, -1, -1):
             for way in range(2):
 
                 @pl.when(sends(way, left))
                 def _():
+                    merge(j, left, way)
                     if left + 1 < pencils - 1:
 
                         @pl.when(has_previous(way))
@@ -501,7 +582,8 @@
             finish(j - 1)
     finish(chunks - 1)
     for j in range(chunks):
-        across(j).wait_send()
+        for i in range(pencils):
+            across(j, i).wait_send()
         for left in range(pencils - 1):
             for way in range(2):
 
@@ -518,15 +600,15 @@
 WHOLE = pl.BlockSpec(memory_space=pltpu.VMEM)
 
 
-def gathered(piece, flag, table, pencils):
+def gathered(piece, table, pencils):
     _, slab, plane = piece.shape
     grid, lanes = slab * pencils, plane // CHUNKS
     fields = (CHUNKS, pencils, 2, slab, lanes)
-    spectrum = (CHUNKS, 2, grid, lanes)
+    spectrum = (2, grid, plane // grid, -(-grid // LANES) * LANES)
     dma = pltpu.SemaphoreType.DMA
     return pl.pallas_call(
         functools.partial(gather_kernel, pencils),
-        in_specs=[SCALARS, WHOLE, WHOLE, ANY],
+        in_specs=[WHOLE, WHOLE, ANY],
         out_specs=[ANY] * 3,
         out_shape=[jax.ShapeDtypeStruct(s, jnp.float32) for s in (fields, fields, spectrum)],
         scratch_shapes=[pltpu.VMEM(s, jnp.float32) for s in (fields, fields, spectrum)]
@@ -543,24 +625,24 @@
         compiler_params=pltpu.CompilerParams(
             collective_id=0, has_side_effects=True, vmem_limit_bytes=VMEM
         ),
-    )(flag, *table, piece)
-
-
-def scattered(potential, own, far, flag, table, pencils):
+    )(*table, piece)
+
+
+def scattered(potential, own, far, table, pencils):
     _, _, _, slab, lanes = own.shape
     dma = pltpu.SemaphoreType.DMA
     arrived = (CHUNKS, 2, pencils - 1, 2, slab, lanes)
     shapes = (potential.shape, own.shape, own.shape, own.shape, arrived)
     return pl.pallas_call(
         functools.partial(scatter_kernel, pencils),
-        in_specs=[SCALARS, WHOLE, WHOLE] + [ANY] * 3,
+        in_specs=[WHOLE, WHOLE] + [ANY] * 3,
         out_specs=ANY,
         out_shape=jax.ShapeDtypeStruct((2, slab, lanes * CHUNKS), jnp.float32),
         scratch_shapes=[pltpu.VMEM(s, jnp.float32) for s in shapes]
         + [
             dma((3, CHUNKS)),
-            dma((CHUNKS,)),
-            dma((CHUNKS,)),
+            dma((pencils, CHUNKS)),
+            dma((pencils, CHUNKS)),
             dma((2, pencils - 1, CHUNKS)),
             dma((2, pencils - 1, CHUNKS)),
             dma((CHUNKS,)),
@@ -568,7 +650,7 @@
         compiler_params=pltpu.CompilerParams(
             collective_id=1, has_side_effects=True, vmem_limit_bytes=VMEM
         ),
-    )(flag, *table, potential, own, far)
+    )(*table, potential, own, far)
 
 
 def schedule(kpts, bands, sets):
@@ -623,13 +705,11 @@
 
     scale = -1.0 / (count * grid**3)
 
-    if pencils == 4 and slab % 8 == 0:
-        own, other, spectrum = gathered(orbitals[:, 0, 0], flag, all_tables[0], pencils)
-        spectrum = spectrum.reshape(CHUNKS, 2, grid, part, grid)
-        spectrum = jnp.pad(spectrum, ((0, 0),) * 4 + ((0, padded - grid),))
-        potential = filtered([spectrum], shift, all_tables, grid, scale)[0]
-        potential = potential[..., :grid].reshape(CHUNKS, 2, grid, lanes)
-        result = scattered(potential, own, other, flag, all_tables[1], pencils)
+    step = math.lcm(grid, LANES)
+    if pencils == 4 and slab % 8 == 0 and lanes % step == 0 and part % 8 == 0:
+        own, other, spectrum = gathered(orbitals[:, 0, 0], all_tables[0], pencils)
+        potential = filtered([spectrum[None]], kcoords, all_tables, grid, scale)[0]
+        result = scattered(potential[0], own, other, all_tables[1], pencils)
         return result[:, None, None]
 
     own_chunks, far_chunks, spectra = [], [], []

time: 340 us -> 291 us (0.86)
  local copies, waits for them, and re-layouts: 34.3 us -> 2.8 us
  Pallas kernels: 300 us -> 288 us
    reshape x2 -> x0, local copies, waits for them, and re-layouts: 21.1 us -> none  [the longest x1 11.1 us: body(): spectrum = spectrum.reshape(CHUNKS, 2, grid, part, grid)]
    pallas_call x2, Pallas kernels: 273 us -> 260 us  [the longest x1 130 us: gathered(): pl.pallas_call(functools.partial(gather_kernel, pencils), in_specs=[WHOLE...]
    pad x1 -> x0, local copies, waits for them, and re-layouts: 7.92 us -> none  [body(): spectrum = jnp.pad(spectrum, ((0, 0),) * 4 + ((0, padded - grid),))]
where the time goes in v3:
time: 291 us
  Pallas kernels  288 us (99%)
    pallas_call x1, Pallas kernels, gathered(): pl.pallas_call(functools.partial(gather_kernel, pencils), in_specs=[WHOLE...  130 us
    pallas_call x1, Pallas kernels, scattered(): pl.pallas_call(functools.partial(scatter_kernel, pencils), in_specs=[WHOL...  130 us
    pallas_call x1, Pallas kernels, filtered(): pl.pallas_call(functools.partial(filter_kernel, grid, scale), grid=(grid...  27.7 us

profile of v3, /device:TPU:0, one launch (start us, length us, event | category | flops | bytes accessed | tf_op | source)
XLA Modules:
  0.0 290.9 jit_solution(17247533564724091089)
XLA Ops:
  0.0 130.4 %shard_map.100 = (f32[6,4,2,24,1536]{4,3,2,1,0:T(8,128)}, f32[6,4,2,24,1536]{4,3,2,1,0:T(8,128)}, f32[2,96,96,128]{3,2,1,0:T(8,128)}) custom-call(bf16[192,192]{1,0:T(8,128)(2,1)} %constant.16.clone.high_ref.refs_0_, bf16[192,192]{1,0:T(8,128)(2,1)} %constant.17.clone.low_ref.refs_1_, f32[2,24,9216]{2,1,0:T(8,128)} %bitcast.9), custom_call_target="tpu_custom_call" | custom-call | tf_op jit(solution)/shard_map/pallas_call | solution.py:609
  130.4 27.7 %shard_map.101 = f32[1,2,96,96,128]{4,3,2,1,0:T(8,128)} custom-call(s32[4,3]{1,0:T(4,128)} %shift_ref.1, bf16[192,192]{1,0:T(8,128)(2,1)} %constant.16.clone.high_ref.refs_0_, bf16[192,192]{1,0:T(8,128)(2,1)} %constant.17.clone.low_ref.refs_1_, bf16[192,192]{1,0:T(8,128)(2,1)} %constant.18.clone.refs_2_.high_ref, ...), custom_call_target="tpu_custom_call" | custom-call | tf_op jit(solution)/shard_map/pallas_call | solution.py:214
  158.2 130.0 %shard_map.102 = f32[2,24,9216]{2,1,0:T(8,128)} custom-call(bf16[192,192]{1,0:T(8,128)(2,1)} %constant.18.clone.refs_2_.high_ref, bf16[192,192]{1,0:T(8,128)(2,1)} %constant.19.clone.refs_3_.low_ref, f32[2,96,96,128]{3,2,1,0:T(8,128)} %bitcast.6, f32[6,4,2,24,1536]{4,3,2,1,0:T(8,128)} %get-tuple-element.9.own_in, f32[6,4,2,24,1536]{4,3,2,1,0:T(8,128)} %get-tuple-element.10.far_in), custom_call_target="tpu_custom_call" | custom-call | tf_op jit(solution)/shard_map/pallas_call | solution.py:636
  288.1 2.8 copy.13
